TPU v7x, 32 devices: a whole 2x2x4 slice. The times are simulated.
32 devices in a mesh: dp: 2 (over core), row: 4 (over y, x), col: 4 (over z).
Axes of the slice: x: 2, y: 2, z: 4, core: 2. Of those that a mesh axis runs over, the one named last changes fastest.
Arguments:
- hidden_in: bfloat16 [32, 768, 1024], P(('dp', 'col'), 'row'), may hold values from -6 to 6
- lengths: int32 [32], P(('dp', 'col')), may hold values from 256 to 1024, as said below
- w_qkv: bfloat16 [768, 3, 768], P('col', None, 'row'), may hold values from -0.21875 to 0.21875
- w_out: bfloat16 [768, 768], P('row', 'col'), may hold values from -1.75 to 1.75
- w_gate_up: bfloat16 [768, 2, 2048], P('col', None, 'row'), may hold values from -0.21875 to 0.21875
- w_down: bfloat16 [2048, 768], P('row', 'col'), may hold values from -0.125 to 0.125
- gain_attn: bfloat16 [768], P('row'), may hold values from 0.5 to 1.5
- gain_mlp: bfloat16 [768], P('row'), may hold values from 0.5 to 1.5
- cotangent: bfloat16 [32, 768, 1024], P(('dp', 'col'), 'row'), may hold values from -6 to 6
Outputs:
- block_out: bfloat16 [32, 768, 1024], P(('dp', 'col'), 'row')
- d_hidden_in: float32 [32, 768, 1024], P(('dp', 'col'), 'row')
- grad_qkv: float32 [768, 3, 768], P('col', None, 'row')
- grad_out: float32 [768, 768], P('row', 'col')
- grad_gate_up: float32 [768, 2, 2048], P('col', None, 'row')
- grad_down: float32 [2048, 768], P('row', 'col')
- grad_gain_attn: float32 [768], P('row')
- grad_gain_mlp: float32 [768], P('row')
Inputs may be any that keep to these rules, and one draw needn't show every extreme that they name: `lengths`: each sequence's count of real tokens; slots from that count on are padding; some sequence is full and some holds exactly 256 tokens.
All inputs are finite; a program needn't handle non-finite values.
Results may differ from a plain program's by a relative error of at most 0.018.
Values may be sent and summed in bfloat16 or wider, within the bound.
A program may use at most 192 MiB of HBM per device.

v0:
```python
import math

import jax
import jax.numpy as jnp
from jax import lax
from jax.sharding import PartitionSpec as P

D = 768
HEAD_DIM = 64


EPS = 1e-05


def rope_tables(length):
    half_dim = HEAD_DIM // 2
    frequency = jnp.exp(
        jnp.arange(half_dim, dtype=jnp.float32) * (-2.0 * math.log(10000.0) / HEAD_DIM)
    )
    angles = jnp.arange(length, dtype=jnp.float32)[:, None] * frequency[None, :]
    return (jnp.cos(angles)[:, None, :], jnp.sin(angles)[:, None, :])


def rotate(values, cos_table, sin_table):
    half_dim = values.shape[-1] // 2
    first_half = values[..., :half_dim]
    second_half = values[..., half_dim:]
    return jnp.concatenate(
        [
            first_half * cos_table - second_half * sin_table,
            second_half * cos_table + first_half * sin_table,
        ],
        axis=-1,
    )


def unrotate(incoming, cos_table, sin_table):
    half_dim = incoming.shape[-1] // 2
    first_half = incoming[..., :half_dim]
    second_half = incoming[..., half_dim:]
    return jnp.concatenate(
        [
            first_half * cos_table + second_half * sin_table,
            second_half * cos_table - first_half * sin_table,
        ],
        axis=-1,
    )


def visible(first_row, row_count, length, valid_len):
    query_pos = first_row + jnp.arange(row_count, dtype=jnp.int32)
    key_pos = jnp.arange(length, dtype=jnp.int32)
    return (key_pos[None, :] <= query_pos[:, None]) & (key_pos[None, :] < valid_len)


def attend(queries, key_rot, values, lengths):
    seq_count, length, head_count, head_size = queries.shape
    block_rows = min(512, length)
    blocks = length // block_rows
    scaling = 1.0 / math.sqrt(head_size)
    flat_q = queries.reshape(seq_count * blocks, block_rows, head_count, head_size)

    def per_block(position):
        seq_id = position // blocks
        first_row = position % blocks * block_rows
        scores = (
            jnp.einsum(
                "qhe,khe->hqk",
                flat_q[position],
                key_rot[seq_id],
                preferred_element_type=jnp.float32,
            )
            * scaling
        )
        allowed = visible(first_row, block_rows, length, lengths[seq_id])
        scores = jnp.where(allowed[None], scores, -1e30)
        highest = jnp.max(scores, axis=-1, keepdims=True)
        exp_sum = jnp.sum(jnp.exp(scores - highest), axis=-1, keepdims=True)
        log_total = highest + jnp.log(exp_sum)
        probs_low = jnp.exp(scores - log_total).astype(jnp.bfloat16)
        mixed_out = jnp.einsum(
            "hqk,khe->qhe", probs_low, values[seq_id], preferred_element_type=jnp.float32
        )
        return (mixed_out.astype(jnp.bfloat16), log_total[..., 0])

    mixed_out, log_totals = lax.map(per_block, jnp.arange(seq_count * blocks, dtype=jnp.int32))
    return (mixed_out.reshape(seq_count, length, head_count * head_size), log_totals)


def attend_back(queries, key_rot, values, lengths, log_totals, d_mixed):
    seq_count, length, head_count, head_size = queries.shape
    block_rows = min(512, length)
    blocks = length // block_rows
    scaling = 1.0 / math.sqrt(head_size)

    def per_sequence(seq_id):
        q_seq = queries[seq_id]
        k_seq = key_rot[seq_id]
        v_seq = values[seq_id]
        d_seq = d_mixed[seq_id]
        d_keys = jnp.zeros((length, head_count, head_size), jnp.float32)
        d_values = jnp.zeros((length, head_count, head_size), jnp.float32)
        query_parts = []
        for block_id in range(blocks):
            first_row = block_id * block_rows
            q_blk = q_seq[first_row : first_row + block_rows]
            d_blk = d_seq[first_row : first_row + block_rows]
            scores = (
                jnp.einsum("qhe,khe->hqk", q_blk, k_seq, preferred_element_type=jnp.float32)
                * scaling
            )
            allowed = visible(first_row, block_rows, length, lengths[seq_id])
            scores = jnp.where(allowed[None], scores, -1e30)
            probs = jnp.exp(scores - log_totals[seq_id * blocks + block_id][..., None])
            d_probs = jnp.einsum("qhe,khe->hqk", d_blk, v_seq, preferred_element_type=jnp.float32)
            inner = jnp.sum(d_probs * probs, axis=-1, keepdims=True)
            d_scores = (probs * (d_probs - inner)).astype(jnp.bfloat16)
            query_parts.append(
                jnp.einsum("hqk,khe->qhe", d_scores, k_seq, preferred_element_type=jnp.float32)
                * scaling
            )
            d_keys = (
                d_keys
                + jnp.einsum("hqk,qhe->khe", d_scores, q_blk, preferred_element_type=jnp.float32)
                * scaling
            )
            d_values = d_values + jnp.einsum(
                "hqk,qhe->khe",
                probs.astype(jnp.bfloat16),
                d_blk,
                preferred_element_type=jnp.float32,
            )
        return (jnp.concatenate(query_parts, axis=0), d_keys, d_values)

    return lax.map(per_sequence, jnp.arange(seq_count, dtype=jnp.int32))


def row_total(values):
    return lax.psum(values, "row")


def all_features(values):
    return lax.all_gather(values, "row", axis=1, tiled=True)


def project_back(weight_whole, operand, equation):
    return lax.psum_scatter(
        jnp.einsum(equation, weight_whole, operand, preferred_element_type=jnp.float32),
        "row",
        scatter_dimension=0,
        tiled=True,
    ).T


def gather_weights(w_qkv, w_out, w_gate_up, w_down, gain_attn, gain_mlp):
    qkv_whole, out_whole, gu_whole, down_whole = (
        lax.all_gather(w_qkv, "col", axis=0, tiled=True),
        lax.all_gather(w_out, "col", axis=1, tiled=True),
        lax.all_gather(w_gate_up, "col", axis=0, tiled=True),
        lax.all_gather(w_down, "col", axis=1, tiled=True),
    )
    return (qkv_whole, out_whole, gu_whole, down_whole, gain_attn, gain_mlp)


def norm_back(d_normed, values, inverse, gain):
    unit = values * inverse[:, None]
    d_unit = d_normed * gain
    inner = row_total(jnp.sum(d_unit * unit, axis=1)) / D
    return (inverse[:, None] * (d_unit - unit * inner[:, None]), jnp.sum(d_normed * unit, axis=0))


def shards(hidden_in, lengths, w_qkv, w_out, w_gate_up, w_down, gain_attn, gain_mlp, cotangent):
    inputs_fm, d_final_fm = (hidden_in, cotangent)
    inputs = inputs_fm.transpose(0, 2, 1)
    d_final = d_final_fm.transpose(0, 2, 1)
    seq_count, length, width_here = inputs.shape
    tokens = seq_count * length
    heads_here = width_here // HEAD_DIM
    qkv_whole, out_whole, gu_whole, down_whole, gain_one, gain_two = gather_weights(
        w_qkv, w_out, w_gate_up, w_down, gain_attn, gain_mlp
    )
    gain_one = gain_one.astype(jnp.float32)
    gain_two = gain_two.astype(jnp.float32)
    cos_table, sin_table = rope_tables(length)
    token_rows = inputs.reshape(tokens, width_here).astype(jnp.float32)
    inv_one = lax.rsqrt(row_total(jnp.sum(token_rows * token_rows, axis=1)) / D + EPS)
    normed_one = (token_rows * inv_one[:, None] * gain_one).astype(jnp.bfloat16)
    full_one = all_features(normed_one)
    projected = jnp.einsum("td,dcf->tcf", full_one, qkv_whole, preferred_element_type=jnp.float32)
    shaped = projected.reshape(seq_count, length, 3, heads_here, HEAD_DIM)
    queries = rotate(shaped[:, :, 0], cos_table, sin_table).astype(jnp.bfloat16)
    key_rot = rotate(shaped[:, :, 1], cos_table, sin_table).astype(jnp.bfloat16)
    values_in = shaped[:, :, 2].astype(jnp.bfloat16)
    attended, log_totals = attend(queries, key_rot, values_in, lengths)
    attn_rows = attended.reshape(tokens, width_here)
    middle = token_rows + project_back(out_whole, attn_rows, "ic,ti->ct")
    inv_two = lax.rsqrt(row_total(jnp.sum(middle * middle, axis=1)) / D + EPS)
    normed_two = (middle * inv_two[:, None] * gain_two).astype(jnp.bfloat16)
    full_two = all_features(normed_two)
    gate_up = jnp.einsum("td,dcf->tcf", full_two, gu_whole, preferred_element_type=jnp.float32)
    gate_pre = gate_up[:, 0]
    up_pre = gate_up[:, 1]
    sigmoid_gate = jax.nn.sigmoid(gate_pre)
    silu_gate = gate_pre * sigmoid_gate
    hidden_act = (silu_gate * up_pre).astype(jnp.bfloat16)
    final = middle + project_back(down_whole, hidden_act, "ic,ti->ct")
    qkv_whole, out_whole, gu_whole, down_whole, gain_one, gain_two = gather_weights(
        w_qkv, w_out, w_gate_up, w_down, gain_attn, gain_mlp
    )
    gain_one = gain_one.astype(jnp.float32)
    gain_two = gain_two.astype(jnp.float32)
    d_out_rows = d_final.reshape(tokens, width_here).astype(jnp.float32)
    d_full_two = all_features(d_final.reshape(tokens, width_here))
    grad_down = jnp.einsum("td,tf->df", d_full_two, hidden_act, preferred_element_type=jnp.float32)
    d_hidden = jnp.einsum("td,fd->tf", d_full_two, down_whole, preferred_element_type=jnp.float32)
    d_gate = d_hidden * up_pre * (sigmoid_gate * (1.0 + gate_pre * (1.0 - sigmoid_gate)))
    d_upward = d_hidden * silu_gate
    d_gate_up = jnp.stack([d_gate, d_upward], axis=1).astype(jnp.bfloat16)
    grad_gate_up = jnp.einsum(
        "td,tcf->dcf", full_two, d_gate_up, preferred_element_type=jnp.float32
    )
    d_normed_two = project_back(gu_whole, d_gate_up, "cjf,tjf->ct")
    d_norm_mid, grad_gain_two = norm_back(d_normed_two, middle, inv_two, gain_two)
    d_middle = d_out_rows + d_norm_mid
    d_full_one = all_features(d_middle.astype(jnp.bfloat16))
    grad_out = jnp.einsum("td,ti->di", d_full_one, attn_rows, preferred_element_type=jnp.float32)
    d_attended = jnp.einsum("td,id->ti", d_full_one, out_whole, preferred_element_type=jnp.float32)
    d_attended = d_attended.astype(jnp.bfloat16).reshape(seq_count, length, heads_here, HEAD_DIM)
    d_queries, d_keys, d_values = attend_back(
        queries, key_rot, values_in, lengths, log_totals, d_attended
    )
    d_projected = jnp.stack(
        [
            unrotate(d_queries, cos_table, sin_table),
            unrotate(d_keys, cos_table, sin_table),
            d_values,
        ],
        axis=2,
    )
    d_projected = d_projected.astype(jnp.bfloat16).reshape(tokens, 3, width_here)
    grad_qkv = jnp.einsum("td,tcf->dcf", full_one, d_projected, preferred_element_type=jnp.float32)
    d_normed_one = project_back(qkv_whole, d_projected, "cjf,tjf->ct")
    d_norm_in, grad_gain_one = norm_back(d_normed_one, token_rows, inv_one, gain_one)
    d_rows = d_middle + d_norm_in
    final_fm = final.reshape(seq_count, length, width_here).transpose(0, 2, 1)
    d_rows_fm = d_rows.reshape(seq_count, length, width_here).transpose(0, 2, 1)
    share_qkv, share_out, share_gu, share_down = (grad_qkv, grad_out, grad_gate_up, grad_down)
    share_gain_one, share_gain_two = (grad_gain_one, grad_gain_two)
    block_out = final_fm.astype(jnp.bfloat16)
    share_qkv, share_out, share_gu, share_down = (
        lax.psum_scatter(
            share_qkv.astype(jnp.bfloat16), "col", scatter_dimension=0, tiled=True
        ).astype(jnp.float32),
        lax.psum_scatter(
            share_out.astype(jnp.bfloat16), "col", scatter_dimension=0, tiled=True
        ).astype(jnp.float32),
        lax.psum_scatter(
            share_gu.astype(jnp.bfloat16), "col", scatter_dimension=0, tiled=True
        ).astype(jnp.float32),
        lax.psum_scatter(
            share_down.astype(jnp.bfloat16), "col", scatter_dimension=0, tiled=True
        ).astype(jnp.float32),
    )
    share_qkv, share_out, share_gu, share_down, share_gain_one, share_gain_two = (
        lax.psum(share_qkv.astype(jnp.bfloat16), "dp").astype(jnp.float32),
        lax.psum(share_out.astype(jnp.bfloat16), "dp").astype(jnp.float32),
        lax.psum(share_gu.astype(jnp.bfloat16), "dp").astype(jnp.float32),
        lax.psum(share_down.astype(jnp.bfloat16), "dp").astype(jnp.float32),
        lax.psum(share_gain_one.astype(jnp.bfloat16), "dp").astype(jnp.float32),
        lax.psum(share_gain_two.astype(jnp.bfloat16), "dp").astype(jnp.float32),
    )
    share_gain_one, share_gain_two = lax.psum((share_gain_one, share_gain_two), "col")
    return (
        block_out,
        d_rows_fm,
        share_qkv,
        share_out.T,
        share_gu,
        share_down.T,
        share_gain_one,
        share_gain_two,
    )


def solution(mesh):
    placed = (
        P(("dp", "col"), "row", None),
        P(("dp", "col")),
        P("col", None, "row"),
        P("row", "col"),
        P("col", None, "row"),
        P("row", "col"),
        P("row"),
        P("row"),
        P(("dp", "col"), "row", None),
    )
    return jax.shard_map(
        shards,
        mesh=mesh,
        in_specs=placed,
        out_specs=(
            P(("dp", "col"), "row", None),
            P(("dp", "col"), "row", None),
            P("col", None, "row"),
            P("row", "col"),
            P("col", None, "row"),
            P("row", "col"),
            P("row"),
            P("row"),
        ),
        check_vma=False,
    )
```

profile of v0, /device:TPU:0, one launch (start us, length us, event | category | flops | bytes accessed | tf_op | source)
XLA Modules:
  0.0 1368.1 jit_solution(13158132489853805055)
XLA Ops:
  11.7 17.5 %psum.84 = f32[4096]{0:T(1024)S(1)} all-reduce(f32[4096]{0:T(1024)S(1)} %bitcast.331), channel_id=1, replica_groups=mesh['dp'=2,'row'=4,'col'=4] {'row'}, use_global_device_ids=true, to_apply=%region_1.0 | all-reduce | flops 4096 | bytes 32768 | tf_op jit(solution)/shard_map/psum | solution.py:139
  33.2 27.9 %all_gather.29 = bf16[768,3,192]{2,1,0:T(4,128)(2,1)S(1)} all-gather(bf16[192,3,192]{2,1,0:T(4,128)(2,1)S(1)} %copy.64), channel_id=1, replica_groups=mesh['dp'=2,'row'=4,'col'=4] {'col'}, dimensions={0}, use_global_device_ids=true | all-gather | bytes 1105920 | tf_op jit(solution)/shard_map/all_gather | solution.py:157
  62.0 14.4 %all_gather.30 = bf16[192,768]{0,1:T(8,128)(2,1)S(1)} all-gather(bf16[192,192]{0,1:T(8,128)(2,1)S(1)} %copy.73), channel_id=1, replica_groups=mesh['dp'=2,'row'=4,'col'=4] {'col'}, dimensions={1}, use_global_device_ids=true | all-gather | bytes 368640 | tf_op jit(solution)/shard_map/all_gather | solution.py:158
  77.0 25.4 %all-gather.6.cloned.1.call-done = bf16[4096,768]{0,1:T(8,128)(2,1)} async-done(((bf16[4096,192]{0,1:T(8,128)(2,1)}), bf16[4096,768]{0,1:T(8,128)(2,1)}) %all-gather.6.cloned.1.call-update) | async-done | bytes 6291472 | tf_op jit(solution)/shard_map/all_gather | solution.py:143
  111.4 12.7 reshape.274
  145.2 115.3 %while.30 = (s32[]{:T(128)}, bf16[8,512,3,64]{1,3,2,0:T(8,128)(2,1)}, f32[8,3,512]{2,1,0:T(4,128)}, s32[8]{0:T(128)S(1)}, bf16[4,1024,3,64]{1,3,2,0:T(8,128)(2,1...) while((s32[]{:T(128)}, ...), condition=%wide.region_5.6_spmd, body=%wide.region_2.5_spmd.sunk | while | flops 421101600 | bytes 22208972 | solution.py:86
  273.4 118.5 %reduce-scatter.11.cloned.1.call-done = f32[192,4096]{1,0:T(8,128)} async-done(((f32[768,4096]{1,0:T(8,128)}), f32[192,4096]{1,0:T(8,128)}) %reduce-scatter.11.cloned.1.call-update) | async-done | bytes 3145744 | tf_op jit(solution)/shard_map/reduce_scatter | solution.py:147
  395.2 15.7 %psum.85 = f32[4096]{0:T(1024)} all-reduce(f32[4096]{0:T(1024)S(1)} %get-tuple-element.382), channel_id=1, replica_groups=mesh['dp'=2,'row'=4,'col'=4] {'row'}, use_global_device_ids=true, to_apply=%region_8.9 | all-reduce | flops 4096 | bytes 32768 | tf_op jit(solution)/shard_map/psum | solution.py:139
  416.8 19.1 %all_gather.33 = bf16[512,768]{0,1:T(8,128)(2,1)} all-gather(bf16[512,192]{0,1:T(8,128)(2,1)} %param.18), channel_id=1, replica_groups=mesh['dp'=2,'row'=4,'col'=4] {'col'}, dimensions={1}, use_global_device_ids=true | all-gather | bytes 983040 | tf_op jit(solution)/shard_map/all_gather | solution.py:160
  435.9 47.9 %all-gather.8.cloned.1.call-done = bf16[4096,768]{0,1:T(8,128)(2,1)} async-done(((bf16[4096,192]{0,1:T(8,128)(2,1)}), bf16[4096,768]{0,1:T(8,128)(2,1)}) %all-gather.8.cloned.1.call-update) | async-done | bytes 6291472 | tf_op jit(solution)/shard_map/all_gather | solution.py:143
  483.8 13.2 fusion.79
  497.0 58.6 %all-gather.12.cloned.1.call-done = bf16[4096,768]{0,1:T(8,128)(2,1)} async-done(((bf16[4096,192]{0,1:T(8,128)(2,1)}), bf16[4096,768]{0,1:T(8,128)(2,1)}) %all-gather.12.cloned.1.call-update) | async-done | bytes 6291472 | tf_op jit(solution)/shard_map/all_gather | solution.py:143
  555.6 14.5 %fusion.82 = (bf16[4096,1,512]{2,0,1:T(8,128)(2,1)S(1)}, bf16[4096,1,512]{2,0,1:T(8,128)(2,1)S(1)}, bf16[4096,512]{1,0:T(8,128)(2,1)}) fusion(f32[4096,2,512]{2,0,1:T(8,128)} %fusion.79, bf16[4096,768]{0,1:T(8,128)(2,1)} %all-gather.12.cloned.1.call-done, bf16[512,768]{0,1:T(8,128)(2,1)} %all_gather.33), kind=kOutput, calls=%fused_computation.114 | convolution fusion | flops 3252682752 | bytes 36438016 | tf_op jit(solution)/shard_map/td,fd->tf/dot_general | solution.py:215
  582.9 120.7 %reduce-scatter.15.cloned.1.call-done = f32[192,4096]{1,0:T(8,128)} async-done(((f32[768,4096]{1,0:T(8,128)}), f32[192,4096]{1,0:T(8,128)}) %reduce-scatter.15.cloned.1.call-update) | async-done | bytes 3145744 | tf_op jit(solution)/shard_map/reduce_scatter | solution.py:147
  707.9 16.7 %psum.86 = f32[4096]{0:T(1024)} all-reduce(f32[4096]{0:T(1024)} %get-tuple-element.331), channel_id=1, replica_groups=mesh['dp'=2,'row'=4,'col'=4] {'row'}, use_global_device_ids=true, to_apply=%region_12.13 | all-reduce | flops 4096 | bytes 32768 | tf_op jit(solution)/shard_map/psum | solution.py:139
  742.2 11.8 fusion.87
  754.1 46.5 %all-gather.14.cloned.1.call-done = bf16[4096,768]{0,1:T(8,128)(2,1)} async-done(((bf16[4096,192]{0,1:T(8,128)(2,1)}), bf16[4096,768]{0,1:T(8,128)(2,1)}) %all-gather.14.cloned.1.call-update) | async-done | bytes 6291472 | tf_op jit(solution)/shard_map/all_gather | solution.py:143
  807.7 182.0 %while.31 = (s32[]{:T(128)}, f32[4,1024,3,64]{1,3,2,0:T(8,128)}, f32[4,1024,3,64]{1,3,2,0:T(8,128)}, bf16[4,1024,3,64]{1,3,2,0:T(8,128)(2,1)}, s32[4]{0:T(128)S(...) while((s32[]{:T(128)}, f32[4,1024,3,64]{1,3,2,0:T(8,128)}, ...), condition=%wide.region_16.17_spmd, body=%wide.region_13.16_spmd.sunk | while | flops 2063530496 | bytes 134841824 | solution.py:135
  1039.0 30.1 %reduce-scatter.19.cloned.1.call-done = bf16[192,3,192]{2,0,1:T(8,128)(2,1)} async-done(((bf16[768,3,192]{2,0,1:T(8,128)(2,1)}), bf16[192,3,192]{2,0,1:T(8,128)(2,1)}) %reduce-scatter.19.cloned.1.call-update) | async-done | bytes 221200 | tf_op jit(solution)/shard_map/reduce_scatter | solution.py:251
  1069.1 10.5 convolution_bitcast_fusion.1
  1097.0 115.4 %reduce-scatter.17.cloned.1.call-done = f32[192,4096]{1,0:T(8,128)} async-done(((f32[768,4096]{1,0:T(8,128)}), f32[192,4096]{1,0:T(8,128)}) %reduce-scatter.17.cloned.1.call-update) | async-done | bytes 3145744 | tf_op jit(solution)/shard_map/reduce_scatter | solution.py:147
  1217.1 15.4 %psum.87 = f32[4096]{0:T(1024)S(1)} all-reduce(f32[4096]{0:T(1024)S(1)} %get-tuple-element.333), channel_id=1, replica_groups=mesh['dp'=2,'row'=4,'col'=4] {'row'}, use_global_device_ids=true, to_apply=%region_19.20 | all-reduce | flops 4096 | bytes 32768 | tf_op jit(solution)/shard_map/psum | solution.py:139
  1232.6 103.7 %reduce-scatter.13.cloned.1.call-done = f32[192,4096]{1,0:T(8,128)} async-done(((f32[768,4096]{1,0:T(8,128)}), f32[192,4096]{1,0:T(8,128)}) %reduce-scatter.13.cloned.1.call-update) | async-done | bytes 3145744 | tf_op jit(solution)/shard_map/reduce_scatter | solution.py:147
  1348.0 12.2 all-reduce
  (346 shorter events, 440.5 us)
Async XLA Ops:
  8.0 94.4 %all-gather.6.cloned.1.call-start = ((), (), s32[]{:S(2)}) async-start(), calls=%async_computation.8 | async-start | bytes 7864320 | tf_op jit(solution)/shard_map/all_gather | solution.py:143
  32.7 359.1 %reduce-scatter.11.cloned.1.call-start = ((), (), s32[]{:S(2)}) async-start(), calls=%async_computation.9 | async-start | bytes 15728640 | tf_op jit(solution)/shard_map/reduce_scatter | solution.py:147
  77.0 59.4 %copy-start.12 = (f32[1024,32]{0,1:T(8,128)}, f32[1024,32]{0,1:T(8,128)S(1)}, u32[]{:S(2)}) copy-start(f32[1024,32]{0,1:T(8,128)S(1)} %get-tuple-element.415) | copy-start | bytes 393220
  77.0 59.4 %copy-start.14 = (f32[1024,32]{0,1:T(8,128)}, f32[1024,32]{0,1:T(8,128)S(1)}, u32[]{:S(2)}) copy-start(f32[1024,32]{0,1:T(8,128)S(1)} %get-tuple-element.416) | copy-start | bytes 393220
  271.0 164.9 %all-gather.10.cloned.1.call-start = ((), (), s32[]{:S(2)}) async-start(), calls=%async_computation.11 | async-start | bytes 1966080 | tf_op jit(solution)/shard_map/all_gather | solution.py:159
  272.8 211.1 %all-gather.8.cloned.1.call-start = ((), (), s32[]{:S(2)}) async-start(), calls=%async_computation.10 | async-start | bytes 7864320 | tf_op jit(solution)/shard_map/all_gather | solution.py:143
  395.2 330.1 %copy-start.1 = (f32[4096,192]{0,1:T(8,128)}, f32[4096,192]{0,1:T(8,128)S(1)}, u32[]{:S(2)}) copy-start(f32[4096,192]{0,1:T(8,128)S(1)} %get-tuple-element.383) | copy-start | bytes 9437188
  411.6 313.7 %copy-start.17 = (f32[4096]{0:T(1024)}, f32[4096]{0:T(1024)S(1)}, u32[]{:S(2)}) copy-start(f32[4096]{0:T(1024)S(1)} %add_rsqrt_fusion) | copy-start | bytes 49156
  413.9 141.7 %all-gather.12.cloned.1.call-start = ((), (), s32[]{:S(2)}) async-start(), calls=%async_computation.13 | async-start | bytes 7864320 | tf_op jit(solution)/shard_map/all_gather | solution.py:143
  416.7 286.9 %reduce-scatter.15.cloned.1.call-start = ((), (), s32[]{:S(2)}) async-start(), calls=%async_computation.14 | async-start | bytes 15728640 | tf_op jit(solution)/shard_map/reduce_scatter | solution.py:147
  582.9 217.7 %all-gather.14.cloned.1.call-start = ((), (), s32[]{:S(2)}) async-start(), calls=%async_computation.15 | async-start | bytes 7864320 | tf_op jit(solution)/shard_map/all_gather | solution.py:143
  730.4 301.4 %reduce-scatter.25.cloned.1.call-start = ((), (), s32[]{:S(2)}) async-start(), calls=%async_computation.20 | async-start | bytes 983040
  742.1 291.5 %reduce-scatter.23.cloned.1.call-start = ((), (), s32[]{:S(2)}) async-start(), calls=%async_computation.19 | async-start | bytes 1966080 | tf_op jit(solution)/shard_map/reduce_scatter | solution.py:257
  754.0 284.9 %reduce-scatter.21.cloned.1.call-start = ((), (), s32[]{:S(2)}) async-start(), calls=%async_computation.18 | async-start | bytes 491520 | tf_op jit(solution)/shard_map/reduce_scatter | solution.py:254
  1018.2 50.8 %reduce-scatter.19.cloned.1.call-start = ((), (), s32[]{:S(2)}) async-start(), calls=%async_computation.17 | async-start | bytes 1474560 | tf_op jit(solution)/shard_map/reduce_scatter | solution.py:251
  1031.7 57.7 %all-reduce.5.cloned.1.call-start = ((), (), s32[]{:S(2)}) async-start(), calls=%async_computation.21 | async-start | bytes 2097152 | tf_op jit(solution)/shard_map/psum | solution.py:266
  1069.1 143.3 %reduce-scatter.17.cloned.1.call-start = ((), (), s32[]{:S(2)}) async-start(), calls=%async_computation.16 | async-start | bytes 15728640 | tf_op jit(solution)/shard_map/reduce_scatter | solution.py:147
  1079.7 256.6 %reduce-scatter.13.cloned.1.call-start = ((), (), s32[]{:S(2)}) async-start(), calls=%async_computation.12 | async-start | bytes 15728640 | tf_op jit(solution)/shard_map/reduce_scatter | solution.py:147
  1089.4 123.0 %copy-start.22 = (f32[4096]{0:T(1024)S(1)}, f32[4096]{0:T(1024)}, u32[]{:S(2)}) copy-start(f32[4096]{0:T(1024)} %copy-done.21) | copy-start | bytes 49156
  1089.4 123.0 %copy-start.28 = (f32[192]{0:T(256)S(1)}, f32[192]{0:T(256)}, u32[]{:S(2)}) copy-start(f32[192]{0:T(256)} %copy-done.27) | copy-start | bytes 2308
  1097.0 239.3 %copy-start.2 = (f32[4096,192]{0,1:T(8,128)S(1)}, f32[4096,192]{0,1:T(8,128)}, u32[]{:S(2)}) copy-start(f32[4096,192]{0,1:T(8,128)} %copy-done.1) | copy-start | bytes 9437188
  1097.0 239.3 %copy-start.18 = (f32[4096]{0:T(1024)S(1)}, f32[4096]{0:T(1024)}, u32[]{:S(2)}) copy-start(f32[4096]{0:T(1024)} %copy-done.17) | copy-start | bytes 49156
  1097.0 239.3 %copy-start.24 = (f32[4096]{0:T(1024)S(1)}, f32[4096]{0:T(1024)}, u32[]{:S(2)}) copy-start(f32[4096]{0:T(1024)} %copy-done.23) | copy-start | bytes 49156
  1097.0 239.3 %copy-start.26 = (f32[192]{0:T(256)S(1)}, f32[192]{0:T(256)}, u32[]{:S(2)}) copy-start(f32[192]{0:T(256)} %convert_element_type.147) | copy-start | bytes 2308
  (36 other events, 215.4 us)
Sparse Core Ops, SparseCore 0:
  32.9 69.5 all-gather.5
  271.1 120.7 reduce-scatter.10
  730.6 69.9 all-gather.13
  1069.2 18.2 all-reduce.4
  1090.5 121.8 reduce-scatter.16
  1215.4 120.8 reduce-scatter.12
Sparse Core Ops, SparseCore 1:
  273.6 36.9 all-gather.9
  414.0 69.8 all-gather.7
  485.5 70.0 all-gather.11
  582.9 120.6 reduce-scatter.14
  742.2 22.6 reduce-scatter.24
  767.2 34.8 reduce-scatter.22
  1018.3 20.6 reduce-scatter.20
  1041.8 27.2 reduce-scatter.18
where the time goes:
time: 1380 us; the launch traced here: 1370 us
  waiting for transfers between devices  672 us (49%)
  matrix products  282 us (20%)
  blocking collectives  141 us (10%)
  other arithmetic  114 us (8%)
  local copies, waits for them, and re-layouts  98.7 us (7%)
  loops' own time  42.7 us (3%)
  between operations  16.6 us (1%)
    reduce_scatter x4, waiting for transfers between devices, project_back(): lax.psum_scatter(jnp.einsum(equation, weight_whole, operand, preferred_el...  458 us
    all_gather x4, waiting for transfers between devices, all_features(): return lax.all_gather(values, 'row', axis=1, tiled=True)  178 us
    psum x4, blocking collectives, row_total(): return lax.psum(values, 'row')  65.3 us
    dot_general x8, matrix products, per_sequence(): jnp.einsum('qhe,khe->hqk', d_blk, v_seq, preferred_element_type=jnp.float32)  50.6 us
    dot_general x4, matrix products, project_back(): jnp.einsum(equation, weight_whole, operand, preferred_element_type=jnp.fl...  35 us
    another operation x1, loops' own time, attend(): lax.map(per_block, jnp.arange(seq_count * blocks, dtype=jnp.int32))  31.6 us
    convert_element_type x4, other arithmetic, per_sequence(): d_scores = (probs * (d_probs - inner)).astype(jnp.bfloat16)  30.3 us
    reduce_scatter x1, waiting for transfers between devices, shards(): lax.psum_scatter(share_qkv.astype(jnp.bfloat16), 'col', scatter_dimension...  30.1 us
  transfers between devices with their start and end apart: 14, of which 10 were waited for; matrix products, arithmetic and copies ran while one was open for 22% of the time, Pallas kernels for 0%

commit v1 on v0

v1 whole, which is shorter than its diff:
```python
import math

import jax
import jax.numpy as jnp
from jax import lax
from jax.sharding import PartitionSpec as P

EPS = 1e-05
HEAD_DIM = 64
ALL = ("dp", "row", "col")
F32, BF16 = jnp.float32, jnp.bfloat16


def dot(a, b, contract):
    return lax.dot_general(a, b, ((contract[:1], contract[1:]), ((), ())), preferred_element_type=F32)


def rope_tables(length):
    half = HEAD_DIM // 2
    freq = jnp.exp(jnp.arange(half, dtype=F32) * (-2.0 * math.log(10000.0) / HEAD_DIM))
    angles = freq[:, None] * jnp.arange(length, dtype=F32)[None, :]
    return jnp.cos(angles), jnp.sin(angles)


def rope(v, cos, sin, sign):
    parts = v.reshape(-1, 2, HEAD_DIM // 2, v.shape[-1])
    a, b = parts[:, 0], parts[:, 1]
    out = jnp.stack([a * cos - sign * b * sin, b * cos + sign * a * sin], axis=1)
    return out.reshape(v.shape)


def norm(x, gain):
    r = lax.rsqrt(jnp.mean(x * x, axis=0, keepdims=True) + EPS)
    return r, (x * r * gain).astype(BF16)


def norm_back(d_normed, x, r, gain):
    unit = x * r
    d_unit = d_normed * gain
    inner = jnp.mean(d_unit * unit, axis=0, keepdims=True)
    return r * (d_unit - unit * inner), jnp.sum(d_normed * unit, axis=1)


def shards(hidden_in, lengths, w_qkv, w_out, w_gate_up, w_down, gain_attn, gain_mlp, cotangent):
    rows, cols = lax.axis_size("row"), lax.axis_size("col")
    depth, _, wide = w_qkv.shape
    ff = w_gate_up.shape[2]
    me = lax.axis_index("row")
    mine = jnp.concatenate(
        [w_out.T, w_qkv.reshape(depth, 3 * wide), w_gate_up.reshape(depth, 2 * ff), w_down.T], axis=1
    )
    half = depth // 2
    part = lax.dynamic_slice_in_dim(mine, lax.axis_index("dp") * half, half, 0)
    whole = lax.all_gather(part, ALL, axis=0)
    whole = whole.reshape(2, rows, cols, half, -1).transpose(1, 2, 0, 3, 4).reshape(rows, cols * depth, -1)
    gains = lax.all_gather(jnp.stack([gain_attn, gain_mlp]), "row", axis=1, tiled=True).astype(F32)
    gain_one, gain_two = gains[0][:, None], gains[1][:, None]
    x = lax.all_to_all(hidden_in, "row", split_axis=0, concat_axis=1, tiled=True)[0]
    g = lax.all_to_all(cotangent, "row", split_axis=0, concat_axis=1, tiled=True)[0]
    valid = lengths[me]
    length = x.shape[1]
    cos, sin = rope_tables(length)
    x = x.astype(F32)
    r_one, n_one = norm(x, gain_one)
    key_pos = jnp.arange(length)[:, None]
    seen = (key_pos <= key_pos.T) & (key_pos < valid)
    scale = 1.0 / math.sqrt(HEAD_DIM)
    kept, attn = [], []
    heads = wide // HEAD_DIM
    for r in range(rows):
        proj = dot(whole[r][:, wide : 4 * wide], n_one, (0, 0))
        q = rope(proj[:wide], cos, sin, 1.0).astype(BF16).reshape(heads, HEAD_DIM, length)
        k = rope(proj[wide : 2 * wide], cos, sin, 1.0).astype(BF16).reshape(heads, HEAD_DIM, length)
        v = proj[2 * wide :].astype(BF16).reshape(heads, HEAD_DIM, length)
        s = jnp.einsum("hek,heq->hkq", k, q, preferred_element_type=F32) * scale
        s = jnp.where(seen, s, -1e30)
        top = jnp.max(s, axis=1, keepdims=True)
        lse = top + jnp.log(jnp.sum(jnp.exp(s - top), axis=1, keepdims=True))
        p = jnp.exp(s - lse).astype(BF16)
        o = jnp.einsum("hek,hkq->heq", v, p, preferred_element_type=F32).astype(BF16)
        kept.append((q, k, v, lse))
        attn.append(o.reshape(wide, length))
    middle = x
    for r in range(rows):
        middle = middle + dot(whole[r][:, :wide], attn[r], (1, 0))
    r_two, n_two = norm(middle, gain_two)
    final, d_n_two, grads_m = middle, 0.0, []
    for r in range(rows):
        w_gu, w_dn = whole[r][:, 4 * wide : 4 * wide + 2 * ff], whole[r][:, 4 * wide + 2 * ff :]
        gu = dot(w_gu, n_two, (0, 0))
        gate, up = gu[:ff], gu[ff:]
        sig = jax.nn.sigmoid(gate)
        silu = gate * sig
        hid = (silu * up).astype(BF16)
        final = final + dot(w_dn, hid, (1, 0))
        d_hid = dot(w_dn, g, (0, 0))
        d_gu = jnp.concatenate([d_hid * up * sig * (1.0 + gate * (1.0 - sig)), d_hid * silu]).astype(BF16)
        d_n_two = d_n_two + dot(w_gu, d_gu, (1, 0))
        grads_m.append(jnp.concatenate([dot(n_two, d_gu, (1, 1)), dot(g, hid, (1, 1))], axis=1).astype(BF16))
    dv_two, grad_gain_two = norm_back(d_n_two, middle, r_two, gain_two)
    d_middle = g.astype(F32) + dv_two
    d_branch = d_middle.astype(BF16)
    d_n_one, grads = 0.0, []
    for r in range(rows):
        q, k, v, lse = kept[r]
        d_o = dot(whole[r][:, :wide], d_branch, (0, 0)).astype(BF16).reshape(heads, HEAD_DIM, length)
        s = jnp.einsum("hek,heq->hkq", k, q, preferred_element_type=F32) * scale
        p = jnp.exp(jnp.where(seen, s, -1e30) - lse)
        d_p = jnp.einsum("hek,heq->hkq", v, d_o, preferred_element_type=F32)
        inner = jnp.sum(d_p * p, axis=1, keepdims=True)
        d_s = (p * (d_p - inner)).astype(BF16)
        d_q = jnp.einsum("hek,hkq->heq", k, d_s, preferred_element_type=F32) * scale
        d_k = jnp.einsum("heq,hkq->hek", q, d_s, preferred_element_type=F32) * scale
        d_v = jnp.einsum("heq,hkq->hek", d_o, p.astype(BF16), preferred_element_type=F32)
        d_proj = jnp.concatenate(
            [
                rope(d_q.reshape(wide, length), cos, sin, -1.0),
                rope(d_k.reshape(wide, length), cos, sin, -1.0),
                d_v.reshape(wide, length),
            ]
        ).astype(BF16)
        d_n_one = d_n_one + dot(whole[r][:, wide : 4 * wide], d_proj, (1, 0))
        grads.append(
            jnp.concatenate(
                [dot(d_branch, attn[r], (1, 1)).astype(BF16), dot(n_one, d_proj, (1, 1)).astype(BF16), grads_m[r]], axis=1
            )
        )
    dv_one, grad_gain_one = norm_back(d_n_one, x, r_one, gain_one)
    d_x = (d_middle + dv_one).astype(BF16)
    out = lax.all_to_all(final.astype(BF16)[None], "row", split_axis=1, concat_axis=0, tiled=True)
    d_x = lax.all_to_all(d_x[None], "row", split_axis=1, concat_axis=0, tiled=True).astype(F32)
    grad = jnp.stack(grads).reshape(rows, cols, 2, half, -1).transpose(2, 0, 1, 3, 4)
    grad = lax.psum_scatter(grad.reshape(2 * rows * cols * half, -1), ALL, scatter_dimension=0, tiled=True)
    grad = lax.all_gather(grad, "dp", axis=0, tiled=True).astype(F32)
    gain_grads = lax.psum(jnp.stack([grad_gain_one, grad_gain_two]), ALL)
    gain_grads = lax.dynamic_slice_in_dim(gain_grads, me * wide, wide, 1)
    return (
        out,
        d_x,
        grad[:, wide : 4 * wide].reshape(depth, 3, wide),
        grad[:, :wide].T,
        grad[:, 4 * wide : 4 * wide + 2 * ff].reshape(depth, 2, ff),
        grad[:, 4 * wide + 2 * ff :].T,
        gain_grads[0],
        gain_grads[1],
    )


def solution(mesh):
    tokens, wide = P(("dp", "col"), "row", None), P("col", None, "row")
    back, gain = P("row", "col"), P("row")
    return jax.shard_map(
        shards,
        mesh=mesh,
        in_specs=(tokens, P(("dp", "col")), wide, back, wide, back, gain, gain, tokens),
        out_specs=(tokens, tokens, wide, back, wide, back, gain, gain),
        check_vma=False,
    )
```

time: 1380 us -> 718 us (0.52)
  waiting for transfers between devices: 672 us -> 110 us
  blocking collectives: 141 us -> 86.1 us
  loops' own time: 42.7 us -> 0 us
  starting transfers between devices: 0.6 us -> 18.3 us
    reduce_scatter x7 -> x1, waiting for transfers between devices: 494 us -> 21.9 us  [shards(): lax.psum_scatter(grad.reshape(2 * rows * cols * half, -1), ALL, scatter_d...]
    all_gather x5 -> x1, waiting for transfers between devices: 178 us -> 88.2 us  [shards(): whole = lax.all_gather(part, ALL, axis=0)]
    another operation x2 -> x0, loops' own time: 42.7 us -> none  [the longest x1 31.6 us: attend(): lax.map(per_block, jnp.arange(seq_count * blocks, dtype=jnp.int32))]
    all_gather x3 -> x2, blocking collectives: 61.5 us -> 26.5 us  [the longest x1 23.9 us: shards(): lax.all_gather(jnp.stack([gain_attn, gain_mlp]), 'row', axis=1, tiled=True)]
    unnamed x1 -> x12, other arithmetic: 1.79 us -> 24 us
    concatenate x4 -> x5, local copies, waits for them, and re-layouts: 5.73 us -> 27.2 us  [the longest x4 25.9 us: shards(): jnp.concatenate([dot(d_branch, attn[r], (1, 1)).astype(BF16), dot(n_one,...]
    psum x6 -> x1, blocking collectives: 80 us -> 59.5 us  [shards(): gain_grads = lax.psum(jnp.stack([grad_gain_one, grad_gain_two]), ALL)]
    all_to_all x0 -> x4, starting transfers between devices: none -> 18.3 us  [the longest x1 5.18 us: shards(): lax.all_to_all(hidden_in, 'row', split_axis=0, concat_axis=1, tiled=True)[0]]
  transfers between devices with their start and end apart: 14 -> 6, of which waited for: 10 -> 2; matrix products, arithmetic and copies ran while one was open for 22% -> 25% of each run, Pallas kernels for 0% -> 0%
where the time goes in v1:
time: 718 us; the launch traced here: 706 us
  matrix products  269 us (37%)
  waiting for transfers between devices  110 us (15%)
  local copies, waits for them, and re-layouts  104 us (14%)
  other arithmetic  102 us (14%)
  blocking collectives  86.1 us (12%)
  starting transfers between devices  18.3 us (3%)
  between operations  16.4 us (2%)
    dot_general x48, matrix products, dot(): lax.dot_general(a, b, ((contract[:1], contract[1:]), ((), ())), preferred...  124 us
    all_gather x1, waiting for transfers between devices, shards(): whole = lax.all_gather(part, ALL, axis=0)  88.2 us
    psum x1, blocking collectives, shards(): gain_grads = lax.psum(jnp.stack([grad_gain_one, grad_gain_two]), ALL)  59.5 us
    dot_general x4, matrix products, shards(): d_p = jnp.einsum('hek,heq->hkq', v, d_o, preferred_element_type=F32)  54.7 us
    convert_element_type x1, other arithmetic, shards(): d_s = (p * (d_p - inner)).astype(BF16)  42.9 us
    unnamed x308, local copies, waits for them, and re-layouts  37.6 us
    dot_general x4, matrix products, shards(): s = jnp.einsum('hek,heq->hkq', k, q, preferred_element_type=F32) * scale  35.3 us
    concatenate x4, local copies, waits for them, and re-layouts, shards(): jnp.concatenate([dot(d_branch, attn[r], (1, 1)).astype(BF16), dot(n_one,...  25.9 us
  transfers between devices with their start and end apart: 6, of which 2 were waited for; matrix products, arithmetic and copies ran while one was open for 25% of the time, Pallas kernels for 0%

profile of v1, /device:TPU:0, one launch (start us, length us, event | category | flops | bytes accessed | tf_op | source)
XLA Modules:
  0.0 705.9 jit_solution(16138932549232344050)
XLA Ops:
  12.7 5.2 all-to-all-start
  17.9 23.9 %all-gather.1 = bf16[4,192,2]{1,2,0:T(2,128)(2,1)S(1)} all-gather(bf16[1,192,2]{1,2,0:T(2,128)(2,1)S(1)} %maximum_bitcast_fusion), channel_id=1, replica_groups=mesh['dp'=2,'row'=4,'col'=4] {'row'}, dimensions={0}, use_global_device_ids=true | all-gather | bytes 3840 | tf_op jit(solution)/shard_map/all_gather | solution.py:56
  52.4 88.2 %all-gather.4.cloned.1.call-done = bf16[3072,2304]{1,0:T(8,128)(2,1)} async-done(((bf16[96,2304]{1,0:T(8,128)(2,1)}), bf16[3072,2304]{1,0:T(8,128)(2,1)}) %all-gather.4.cloned.1.call-update) | async-done | bytes 14155792 | tf_op jit(solution)/shard_map/all_gather | solution.py:54
  140.6 5.8 fusion.116
  160.5 7.0 fusion.123
  168.9 7.1 %fusion.3 = (f32[3,1024]{1,0:T(4,128)S(1)}, f32[3,1024]{1,0:T(4,128)S(1)}, f32[3,1024,1024]{2,1,0:T(8,128)}) fusion(pred[1024,1024]{1,0:T(8,128)(4,1)S(1)} %fusion.8, f32[3,1024,1024]{2,1,0:T(8,128)S(1)} %fusion.122, bf16[3,64,1024]{2,1,0:T(8,128)(2,1)S(1)} %bitcast.297, bf16[3,64,1024]{2,1,0:T(8,128)(2,1)S(1)} %bitcast.299), kind=kOutput, calls=%fused_computation.24 | convolution fusion | flops 421521408 | bytes 27025408 | tf_op jit(solution)/shard_map/hek,heq->hkq/dot_general | solution.py:75
  176.1 19.3 %exponential_reduce_fusion = (f32[3,1024]{1,0:T(4,128)S(1)}, f32[3,1024]{1,0:T(4,128)S(1)}, f32[3,1024]{1,0:T(4,128)S(1)}, f32[3,1024]{1,0:T(4,128)S(1)}, f32[3,1024,1024]{2,1,0:T(8,128)}) fusion(f32[3,1024,1024]{2,1,0:T(8,128)} %get-tuple-element.163, f32[3,1024]{1,0:T(4,128)S(1)} %get-tuple-element.68, pred[1024,1024]{1,0:T(8,128)(4,1)S(1)} %fusion.8, ...), kind=kOutput, calls=%fused_computation.10 | convolution fusion | flops 446681088 | bytes 52240384 | tf_op jit(solution)/shard_map/hek,heq->hkq/dot_general | solution.py:75
  195.5 11.6 %exponential_reduce_fusion.2 = (f32[3,1024]{1,0:T(4,128)S(1)}, f32[3,1024]{1,0:T(4,128)S(1)}) fusion(f32[3,1024,1024]{2,1,0:T(8,128)} %get-tuple-element.164, f32[3,1024]{1,0:T(4,128)S(1)} %get-tuple-element.65, pred[1024,1024]{1,0:T(8,128)(4,1)S(1)} %fusion.8, f32[3,1024]{1,0:T(4,128)S(1)} %get-tuple-element.66, f32[3,1024,1024]{2,1,0:T(8,128)} %fusion.123), kind=kLoop, calls=%fused_computation.16 | loop fusion | flops 25159680 | bytes 26263552 | tf_op jit(solution)/shard_map/reduce_sum | solution.py:78
  240.2 5.3 fusion.34
  245.5 5.8 multiply_convert_fusion.8
  308.3 6.4 fusion.124
  319.4 6.4 fusion.125
  330.3 6.4 fusion.126
  341.1 35.5 %multiply_reduce_fusion = (f32[3,1024]{1,0:T(4,128)S(1)}, f32[3,1024]{1,0:T(4,128)S(1)}, f32[3,1024]{1,0:T(4,128)S(1)}, f32[3,1024]{1,0:T(4,128)S(1)}, f32[3,1024,1024]{2,1,0:T(8,128)}) fusion(f32[3,1024,1024]{2,1,0:T(8,128)} %get-tuple-element.163, f32[3,1024]{1,0:T(4,128)S(1)} %log_add_fusion, pred[1024,1024]{1,0:T(8,128)(4,1)S(1)} %copy-done.9, ...), kind=kOutput, calls=%fused_computation.2 | convolution fusion | flops 465555456 | bytes 102596608 | tf_op jit(solution)/shard_map/hek,heq->hkq/dot_general | solution.py:109
  376.6 42.9 %multiply_convert_fusion = (bf16[3,1024,1024]{2,1,0:T(8,128)(2,1)}, bf16[3,1024,1024]{2,1,0:T(8,128)(2,1)}, bf16[3,1024,1024]{2,1,0:T(8,128)(2,1)}, bf16[3,1024,1024]{2,1,0:T(8,128)(2,1)}) fusion(f32[3,1024,1024]{2,1,0:T(8,128)} %get-tuple-element.168, f32[3,1024,1024]{2,1,0:T(8,128)} %get-tuple-element.163, f32[3,1024]{1,0:T(4,128)S(1)} %get-tuple-element.60, ...), kind=kLoop, calls=%fused_computation.1 | loop fusion | flops 75497472 | bytes 126976000 | tf_op jit(solution)/shard_map/convert_element_type | solution.py:111
  491.1 6.9 concatenate.71
  498.0 6.9 concatenate.69
  505.0 6.9 concatenate.72
  511.9 6.0 pad_maximum_fusion
  517.9 5.8 copy.169
  539.3 12.8 %reduce.7 = bf16[768,1024]{1,0:T(8,128)(2,1)} reduce(bf16[768,1,1024]{2,1,0:T(2,128)(2,1)} %bitcast.260, bf16[]{:T(256)} %broadcast.255), dimensions={1}, to_apply=%bitcast.227.reduce_sub_computation | reduce | bytes 3145730
  579.4 11.2 %reduce.8 = bf16[768,1024]{1,0:T(8,128)(2,1)} reduce(bf16[768,1,1024]{2,1,0:T(2,128)(2,1)S(1)} %bitcast.261, bf16[]{:T(256)} %broadcast.255), dimensions={1}, to_apply=%bitcast.226.reduce_sub_computation | reduce | bytes 3145730
  599.1 59.5 %psum.7 = f32[2,768]{1,0:T(2,128)S(1)} all-reduce(f32[2,768]{1,0:T(2,128)S(1)} %pad_maximum_fusion.41), channel_id=1, replica_groups=mesh['dp'=2,'row'=4,'col'=4] {'dp','row','col'}, use_global_device_ids=true, to_apply=%region_19.20 | all-reduce | flops 1536 | bytes 12288 | tf_op jit(solution)/shard_map/psum | solution.py:135
  669.6 21.9 %reduce-scatter.2.cloned.1.call-done = bf16[96,2304]{1,0:T(8,128)(2,1)} async-done(((bf16[3072,2304]{1,0:T(8,128)(2,1)}), bf16[96,2304]{1,0:T(8,128)(2,1)}) %reduce-scatter.2.cloned.1.call-update) | async-done | bytes 442384 | tf_op jit(solution)/shard_map/reduce_scatter | solution.py:133
  (469 shorter events, 274.8 us)
Async XLA Ops:
  7.2 133.4 %all-gather.4.cloned.1.call-start = ((), (), s32[]{:S(2)}) async-start(), calls=%async_computation.6 | async-start | bytes 14598144 | tf_op jit(solution)/shard_map/all_gather | solution.py:54
  10.6 31.3 %copy-start.117 = (s32[4]{0:T(128)S(1)}, s32[4]{0:T(128)}, u32[]{:S(2)}) copy-start(s32[4]{0:T(128)} %param.10) | copy-start | bytes 52
  12.7 32.7 %all-to-all-start = ((bf16[4,192,1024]{2,1,0:T(8,128)(2,1)}), bf16[4,192,1024]{2,1,0:T(8,128)(2,1)S(1)}, u32[]{:S(2)}, u32[]{:S(2)}) async-start(bf16[4,192,1024]{2,1,0:T(8,128)(2,1)} %param.9), calls=%async_computation | async-start | bytes 3145728 | tf_op jit(solution)/shard_map/all_to_all | solution.py:58
  45.0 112.8 %copy-start.35 = (f32[32,1024]{1,0:T(8,128)}, f32[32,1024]{1,0:T(8,128)S(1)}, u32[]{:S(2)}) copy-start(f32[32,1024]{1,0:T(8,128)S(1)} %get-tuple-element.162) | copy-start | bytes 393220
  45.4 183.3 %copy-start.8 = (pred[1024,1024]{1,0:T(8,128)(4,1)}, pred[1024,1024]{1,0:T(8,128)(4,1)S(1)}, u32[]{:S(2)}) copy-start(pred[1024,1024]{1,0:T(8,128)(4,1)S(1)} %fusion.8) | copy-start | bytes 3145732
  45.4 200.1 %all-to-all-start.2 = ((bf16[4,192,1024]{2,1,0:T(8,128)(2,1)}), bf16[4,192,1024]{2,1,0:T(8,128)(2,1)}, u32[]{:S(2)}, u32[]{:S(2)}) async-start(bf16[4,192,1024]{2,1,0:T(8,128)(2,1)} %param.17), calls=%async_computation.2 | async-start | bytes 3145728 | tf_op jit(solution)/shard_map/all_to_all | solution.py:59
  49.8 641.7 %reduce-scatter.2.cloned.1.call-start = ((), (), s32[]{:S(2)}) async-start(), calls=%async_computation.5 | async-start | bytes 14598144 | tf_op jit(solution)/shard_map/reduce_scatter | solution.py:133
  152.0 76.7 %copy-start.41 = (bf16[192,1024]{1,0:T(8,128)(2,1)}, bf16[192,1024]{1,0:T(8,128)(2,1)S(1)}, u32[]{:S(2)}) copy-start(bf16[192,1024]{1,0:T(8,128)(2,1)S(1)} %slice.602) | copy-start | bytes 1179652
  154.2 67.4 %copy-start.37 = (bf16[192,1024]{1,0:T(8,128)(2,1)}, bf16[192,1024]{1,0:T(8,128)(2,1)S(1)}, u32[]{:S(2)}) copy-start(bf16[192,1024]{1,0:T(8,128)(2,1)S(1)} %slice.603) | copy-start | bytes 1179652
  156.4 50.7 %copy-start.39 = (bf16[192,1024]{1,0:T(8,128)(2,1)}, bf16[192,1024]{1,0:T(8,128)(2,1)S(1)}, u32[]{:S(2)}) copy-start(bf16[192,1024]{1,0:T(8,128)(2,1)S(1)} %slice.605) | copy-start | bytes 1179652
  158.5 17.6 %copy-start.43 = (bf16[3,2,32,1024]{3,2,1,0:T(8,128)(2,1)}, bf16[3,2,32,1024]{3,2,1,0:T(8,128)(2,1)S(1)}, u32[]{:S(2)}) copy-start(bf16[3,2,32,1024]{3,2,1,0:T(8,128)(2,1)S(1)} %get-tuple-element.175) | copy-start | bytes 1179652
  160.5 15.6 %copy-start.45 = (bf16[3,2,32,1024]{3,2,1,0:T(8,128)(2,1)}, bf16[3,2,32,1024]{3,2,1,0:T(8,128)(2,1)S(1)}, u32[]{:S(2)}) copy-start(bf16[3,2,32,1024]{3,2,1,0:T(8,128)(2,1)S(1)} %get-tuple-element.176) | copy-start | bytes 1179652
  195.4 11.7 %copy-start.75 = (f32[3,1024]{1,0:T(4,128)}, f32[3,1024]{1,0:T(4,128)S(1)}, u32[]{:S(2)}) copy-start(f32[3,1024]{1,0:T(4,128)S(1)} %log_add_fusion.3) | copy-start | bytes 36868
  195.4 11.8 %copy-start.1 = (f32[3,1024,1024]{2,1,0:T(8,128)S(1)}, f32[3,1024,1024]{2,1,0:T(8,128)}, u32[]{:S(2)}) copy-start(f32[3,1024,1024]{2,1,0:T(8,128)} %copy-done) | copy-start | bytes 37748740
  195.4 18.9 %slice-start.15 = ((s8[12582912]{0:T(1024)(128)(4,1)}), s8[4194304]{0:T(1024)(128)(4,1)S(1)}, s32[]{:S(2)}) async-start(s8[12582912]{0:T(1024)(128)(4,1)} %bitcast.238), calls=%async_computation.22 | async-start | bytes 8388608
  195.5 18.9 %slice-start.16 = ((s8[12582912]{0:T(1024)(128)(4,1)}), s8[4194304]{0:T(1024)(128)(4,1)S(1)}, s32[]{:S(2)}) async-start(s8[12582912]{0:T(1024)(128)(4,1)} %bitcast.238), calls=%async_computation.23 | async-start | bytes 8388608
  207.1 14.5 %copy-start.79 = (f32[3,1024]{1,0:T(4,128)}, f32[3,1024]{1,0:T(4,128)S(1)}, u32[]{:S(2)}) copy-start(f32[3,1024]{1,0:T(4,128)S(1)} %log_add_fusion.1) | copy-start | bytes 36868
  236.1 54.9 %copy-start.2 = (f32[768,1024]{1,0:T(8,128)}, f32[768,1024]{1,0:T(8,128)S(1)}, u32[]{:S(2)}) copy-start(f32[768,1024]{1,0:T(8,128)S(1)} %get-tuple-element.166) | copy-start | bytes 9437188
  290.9 12.9 %slice-start = ((s8[12582912]{0:T(1024)(128)(4,1)}), s8[4194304]{0:T(1024)(128)(4,1)S(1)}, s32[]{:S(2)}) async-start(s8[12582912]{0:T(1024)(128)(4,1)} %bitcast.228), calls=%async_computation.7 | async-start | bytes 8388608
  376.6 42.9 %copy-start.34 = (bf16[3,2,32,1024]{3,2,1,0:T(8,128)(2,1)S(1)}, bf16[3,2,32,1024]{3,2,1,0:T(8,128)(2,1)}, u32[]{:S(2)}) copy-start(bf16[3,2,32,1024]{3,2,1,0:T(8,128)(2,1)} %copy-done.33) | copy-start | bytes 1179652
  452.3 11.3 %copy-start.36 = (f32[32,1024]{1,0:T(8,128)S(1)}, f32[32,1024]{1,0:T(8,128)}, u32[]{:S(2)}) copy-start(f32[32,1024]{1,0:T(8,128)} %copy-done.35) | copy-start | bytes 393220
  452.3 11.3 %copy-start.57 = (f32[32,1024]{1,0:T(8,128)S(1)}, f32[32,1024]{1,0:T(8,128)}, u32[]{:S(2)}) copy-start(f32[32,1024]{1,0:T(8,128)} %get-tuple-element.160) | copy-start | bytes 393220
  556.3 38.4 %all-to-all-start.1 = ((bf16[4,2,98304]{2,1,0:T(2,128)(2,1)}), bf16[4,2,98304]{2,1,0:T(2,128)(2,1)}, u32[]{:S(2)}, u32[]{:S(2)}) async-start(bf16[4,2,98304]{2,1,0:T(2,128)(2,1)} %reshape.376), calls=%async_computation.1 | async-start | bytes 3145728 | tf_op jit(solution)/shard_map/all_to_all | solution.py:130
  594.7 69.4 %all-to-all-start.3 = ((bf16[4,2,98304]{2,1,0:T(2,128)(2,1)}), bf16[4,2,98304]{2,1,0:T(2,128)(2,1)}, u32[]{:S(2)}, u32[]{:S(2)}) async-start(bf16[4,2,98304]{2,1,0:T(2,128)(2,1)} %reshape.374), calls=%async_computation.3 | async-start | bytes 3145728 | tf_op jit(solution)/shard_map/all_to_all | solution.py:131
  (130 other events, 573.6 us)
Sparse Core Ops, SparseCore 0:
  12.8 127.7 all-gather.3
  523.8 167.5 reduce-scatter.1
